TPU v7x, 32 devices: a whole 2x2x4 slice. The times are simulated.
32 devices in a mesh: grp: 2 (over x), exp: 4 (over y, core), base: 4 (over z).
Axes of the slice: x: 2, y: 2, z: 4, core: 2. Of those that a mesh axis runs over, the one named last changes fastest.
Arguments:
- tokens: bfloat16 [512, 7168], P(('grp', 'exp'), 'base'), parts along dimension 0, may hold values from -6 to 6
- expert_ids: int32 [512, 8], P(('grp', 'exp')), parts along dimension 0, may hold values from 0 to 15, all different within a row; in each aligned block of 64 rows (0 to 63, 64 to 127, ...) at most 48 rows name the same one
- gate_q: int32 [512, 8], P(('grp', 'exp')), parts along dimension 0, may hold values from 1 to 65536
- importance: float32 [7168], P('base'), may hold values from 0.5 to 18
- dense_gate: bfloat16 [16, 7168, 1024], P('exp', None, 'base'), may hold values from -0.0625 to 0.0625
- dense_up: bfloat16 [16, 7168, 1024], P('exp', None, 'base'), may hold values from -0.0625 to 0.0625
- dense_down: bfloat16 [16, 1024, 7168], P('exp', None, 'base'), may hold values from -0.1875 to 0.1875
- delta_gate: bfloat16 [16, 7168, 128], P('exp', None, 'base'), may hold values from -0.0625 to 0.0625
- delta_up: bfloat16 [16, 7168, 128], P('exp', None, 'base'), may hold values from -0.0625 to 0.0625
- delta_down: bfloat16 [16, 128, 7168], P('exp', None, 'base'), may hold values from -0.5 to 0.5
- base_gate: bfloat16 [7168, 1024], P(None, 'base'), may hold values from -0.0625 to 0.0625
- base_up: bfloat16 [7168, 1024], P(None, 'base'), may hold values from -0.0625 to 0.0625
- base_down: bfloat16 [1024, 7168], P('base'), may hold values from -0.1875 to 0.1875
Outputs:
- errors: float32 [512], P(('grp', 'exp')), parts along dimension 0
There are 2 independent parts, one for each index of `grp`. A program takes and returns all parts, laid end to end along the dimension named above; an argument that names none is the same for every part. Nothing has to cross between parts.
Inputs may be any that keep to these rules, and one draw needn't show every extreme that they name: `expert_ids`: A token names 8 different experts; among the tokens of one index of exp no expert is named more than 48 times.
All inputs are finite; a program needn't handle non-finite values.
Results may differ from a plain program's by a relative error of at most 0.00064.
Values may be sent and summed in bfloat16 or wider, within the bound.
A program may use at most 256 MiB of HBM per device.

v0:
```python
import jax
import jax.numpy as jnp
from jax import lax
from jax.sharding import PartitionSpec as P

D = 7168


def swiglu(rows, gate_w, up_w):
    gate_pre = jnp.dot(rows, gate_w, preferred_element_type=jnp.float32)
    up_pre = jnp.dot(rows, up_w, preferred_element_type=jnp.float32)
    return (jax.nn.silu(gate_pre) * up_pre).astype(jnp.bfloat16)


def shards(
    tokens,
    expert_ids,
    gate_q,
    importance,
    dense_gate,
    dense_up,
    dense_down,
    delta_gate,
    delta_up,
    delta_down,
    base_gate,
    base_up,
    base_down,
):
    groups = lax.axis_size("exp")
    splits = lax.axis_size("base")
    tok_rows, local_width = tokens.shape
    top_k = expert_ids.shape[1]
    local_experts = dense_gate.shape[0]
    capacity = tok_rows * top_k * 3 // (2 * local_experts * groups)
    dense_width = dense_gate.shape[2]
    low_width = delta_gate.shape[2]
    all_rows = tok_rows * groups
    slots = capacity * groups
    routing = lax.all_gather(
        jnp.concatenate([expert_ids, gate_q], axis=1), "exp", axis=0, tiled=True
    )
    own_rows = lax.all_gather(tokens, "base", axis=1, tiled=True)
    rows = lax.all_gather(own_rows, "exp", axis=0, tiled=True)
    ids, gates = (routing[:, :top_k], routing[:, top_k:])
    first = lax.axis_index("exp") * local_experts
    mine = first + jnp.arange(local_experts, dtype=jnp.int32)
    hit = ids[:, None, :] == mine[None, :, None]
    weight = jnp.sum(jnp.where(hit, gates[:, None, :].astype(jnp.float32), 0.0), axis=2) / 65536.0
    named = jnp.any(hit, axis=2)
    order = jnp.arange(all_rows, dtype=jnp.int32)
    block = order // tok_rows
    before = (block[:, None] == block[None, :]) & (order[None, :] < order[:, None])
    position = jnp.dot(
        before.astype(jnp.bfloat16), named.astype(jnp.bfloat16), preferred_element_type=jnp.float32
    ).astype(jnp.int32)
    slot = jnp.where(named, block[:, None] * capacity + position, -1)
    pick = jnp.arange(slots, dtype=jnp.int32)[None, :, None] == slot.T[:, None, :]
    select = pick.astype(jnp.bfloat16)
    shared = swiglu(own_rows, base_gate, base_up)
    partial_value = jnp.dot(shared, base_down, preferred_element_type=jnp.float32)
    base_own = lax.psum_scatter(
        partial_value.astype(jnp.bfloat16), "base", scatter_dimension=1, tiled=True
    )
    base_all = lax.all_gather(base_own, "exp", axis=0, tiled=True)
    packed = []
    for j in range(local_experts):
        hidden = swiglu(rows, dense_gate[j], dense_up[j])
        low = swiglu(rows, delta_gate[j], delta_up[j])
        both = jnp.concatenate([hidden, low], axis=1)
        packed.append(
            jnp.dot(select[j], both, preferred_element_type=jnp.float32).astype(jnp.bfloat16)
        )
    sent = jnp.stack(packed)
    full = lax.all_gather(sent, "base", axis=0, tiled=False)
    total = jnp.zeros((all_rows,), jnp.float32)
    for j in range(local_experts):
        hid = jnp.concatenate([full[b, j, :, :dense_width] for b in range(splits)], axis=1)
        low = jnp.concatenate([full[b, j, :, dense_width:] for b in range(splits)], axis=1)
        residual = jnp.dot(hid, dense_down[j], preferred_element_type=jnp.float32) - jnp.dot(
            low, delta_down[j], preferred_element_type=jnp.float32
        )
        residual = residual.astype(jnp.bfloat16).astype(jnp.float32)
        base_rows = jnp.dot(select[j], base_all, preferred_element_type=jnp.float32)
        deviation = residual - base_rows
        squares = jnp.sum(importance * deviation * deviation, axis=1)
        back = jnp.sum(jnp.where(pick[j], squares[:, None], 0.0), axis=0)
        total = total + weight[:, j] * back
    total = lax.psum(total / D, ("exp", "base"))
    return lax.dynamic_slice_in_dim(total, lax.axis_index("exp") * tok_rows, tok_rows)


def solution(mesh):
    in_specs = (
        P(("grp", "exp"), "base"),
        P(("grp", "exp"), None),
        P(("grp", "exp"), None),
        P("base"),
        P("exp", None, "base"),
        P("exp", None, "base"),
        P("exp", None, "base"),
        P("exp", None, "base"),
        P("exp", None, "base"),
        P("exp", None, "base"),
        P(None, "base"),
        P(None, "base"),
        P("base", None),
    )
    out_specs = P(("grp", "exp"))
    return jax.shard_map(shards, mesh=mesh, in_specs=in_specs, out_specs=out_specs, check_vma=False)
```

profile of v0, /device:TPU:0, one launch (start us, length us, event | category | flops | bytes accessed | tf_op | source)
XLA Modules:
  0.0 204.3 jit_solution(16887898204992520157)
XLA Ops:
  7.4 23.4 %all_gather.19 = bf16[64,7168]{1,0:T(8,128)(2,1)} all-gather(bf16[64,1792]{1,0:T(8,128)(2,1)} %param.13), channel_id=1, replica_groups=mesh['grp'=2,'exp'=4,'base'=4] {'base'}, dimensions={1}, use_global_device_ids=true | all-gather | bytes 1146880 | tf_op jit(solution)/shard_map/all_gather | solution.py:43
  30.8 0.0 all-gather.5.cloned.1.call-update
  30.8 0.0 reduce-scatter.2.cloned.1.call-start
  30.9 3.1 %fusion.206 = f32[64,256]{1,0:T(8,128)S(1)} fusion(bf16[64,7168]{1,0:T(8,128)(2,1)} %all_gather.19, bf16[7168,256]{1,0:T(8,128)(2,1)} %param.23), kind=kOutput, calls=%fused_computation.267 | convolution fusion | flops 234881024 | bytes 4653056 | tf_op jit(solution)/shard_map/dot_general | solution.py:10
  34.0 6.8 %convolution_convert_fusion = bf16[64,7168]{1,0:T(8,128)(2,1)} fusion(bf16[256,7168]{1,0:T(8,128)(2,1)} %param.25, bf16[64,7168]{1,0:T(8,128)(2,1)S(1)} %copy-done.1, bf16[7168,256]{1,0:T(8,128)(2,1)} %param.24, f32[64,256]{1,0:T(8,128)S(1)} %fusion.206), kind=kOutput, calls=%fused_computation | convolution fusion | flops 470319104 | bytes 9240576 | tf_op jit(solution)/shard_map/dot_general | solution.py:61
  40.8 0.0 reduce-scatter.2.cloned.1.call-update
  40.8 0.0 all-gather.7.cloned.1.call-start
  40.9 5.5 %all-gather.1 = s32[4,64,16]{1,2,0:T(8,128)S(1)} all-gather(s32[1,64,16]{1,2,0:T(8,128)S(1)} %add_bitcast_fusion), channel_id=1, replica_groups=mesh['grp'=2,'exp'=4,'base'=4] {'exp'}, dimensions={0}, use_global_device_ids=true | all-gather | bytes 20480 | tf_op jit(solution)/shard_map/all_gather | solution.py:40
  46.4 0.1 reshape.45
  46.5 0.1 compare_reduce_fusion
  46.6 0.2 fusion.82
  46.9 0.1 iota_compare_fusion
  47.0 15.2 %all-gather.5.cloned.1.call-done = bf16[256,7168]{1,0:T(8,128)(2,1)} async-done(((bf16[64,7168]{1,0:T(8,128)(2,1)}), bf16[256,7168]{1,0:T(8,128)(2,1)}) %all-gather.5.cloned.1.call-update) | async-done | bytes 3670032 | tf_op jit(solution)/shard_map/all_gather | solution.py:44
  62.2 3.4 %fusion.88 = f32[256,32]{0,1:T(8,128)S(1)} fusion(bf16[256,7168]{1,0:T(8,128)(2,1)} %all-gather.5.cloned.1.call-done, bf16[4,7168,32]{1,2,0:T(8,128)(2,1)S(1)} %copy-done.2), kind=kOutput, calls=%fused_computation.97 | convolution fusion | flops 117440512 | bytes 4161536 | tf_op jit(solution)/shard_map/dot_general | solution.py:10
  65.6 0.0 copy-done
  65.6 3.8 %fusion.10 = f32[256,256]{0,1:T(8,128)S(1)} fusion(bf16[256,7168]{1,0:T(8,128)(2,1)S(1)} %copy-done, bf16[4,7168,256]{2,1,0:T(8,128)(2,1)} %param.17), kind=kOutput, calls=%fused_computation.11 | convolution fusion | flops 939524096 | bytes 7602176 | tf_op jit(solution)/shard_map/dot_general | solution.py:10
  69.5 1.2 fusion.80
  70.7 0.0 slice-start.1
  70.7 3.9 %fusion.60 = bf16[256,256]{0,1:T(8,128)(2,1)S(1)} fusion(bf16[256,7168]{1,0:T(8,128)(2,1)S(1)} %copy-done, bf16[4,7168,256]{2,1,0:T(8,128)(2,1)} %param.18, f32[256,256]{0,1:T(8,128)S(1)} %fusion.10), kind=kOutput, calls=%fused_computation.69 | convolution fusion | flops 939917312 | bytes 7733248 | tf_op jit(solution)/shard_map/dot_general | solution.py:11
  74.6 0.2 fusion.75
  74.8 1.2 fusion.91
  76.0 0.0 slice-start.3
  76.0 1.2 fusion.94
  77.2 1.2 fusion.97
  78.4 0.0 slice-done
  78.5 1.6 fusion.14
  80.1 1.6 fusion.18
  81.7 1.2 fusion.79
  82.9 1.2 fusion.78
  84.2 3.9 %fusion.63 = bf16[256,256]{0,1:T(8,128)(2,1)S(1)} fusion(bf16[256,7168]{1,0:T(8,128)(2,1)S(1)} %copy-done, bf16[4,7168,256]{2,1,0:T(8,128)(2,1)} %param.18, f32[256,256]{0,1:T(8,128)S(1)} %fusion.14), kind=kOutput, calls=%fused_computation.70 | convolution fusion | flops 939917312 | bytes 7733248 | tf_op jit(solution)/shard_map/dot_general | solution.py:11
  88.1 3.7 %fusion.66 = bf16[256,256]{0,1:T(8,128)(2,1)S(1)} fusion(bf16[256,7168]{1,0:T(8,128)(2,1)S(1)} %copy-done, bf16[4,7168,256]{2,1,0:T(8,128)(2,1)} %param.18, f32[256,256]{0,1:T(8,128)S(1)} %fusion.18), kind=kOutput, calls=%fused_computation.71 | convolution fusion | flops 939917312 | bytes 7733248 | tf_op jit(solution)/shard_map/dot_general | solution.py:11
  91.8 0.2 fusion.74
  92.1 0.2 fusion.73
  92.3 1.2 fusion.77
  93.5 1.6 fusion.22
  95.1 3.7 %fusion.69 = bf16[256,256]{0,1:T(8,128)(2,1)S(1)} fusion(bf16[256,7168]{1,0:T(8,128)(2,1)S(1)} %copy-done, bf16[4,7168,256]{2,1,0:T(8,128)(2,1)} %param.18, f32[256,256]{0,1:T(8,128)S(1)} %fusion.22), kind=kOutput, calls=%fused_computation.72 | convolution fusion | flops 939917312 | bytes 7733248 | tf_op jit(solution)/shard_map/dot_general | solution.py:11
  98.9 0.2 fusion.72
  99.1 0.9 pad_maximum_fusion
  100.0 0.0 all-gather.7.cloned.1.call-update
  100.1 0.1 fusion.189
  100.2 0.0 reduce-scatter.2.cloned.1.call-done
  100.2 9.8 %all_gather.23 = bf16[256,1792]{1,0:T(8,128)(2,1)S(1)} all-gather(bf16[64,1792]{1,0:T(8,128)(2,1)} %reduce-scatter.2.cloned.1.call-done), channel_id=1, replica_groups=mesh['grp'=2,'exp'=4,'base'=4] {'exp'}, dimensions={0}, use_global_device_ids=true | all-gather | bytes 1146880 | tf_op jit(solution)/shard_map/all_gather | solution.py:65
  110.0 40.2 %all-gather.7.cloned.1.call-done = bf16[16,192,288]{2,1,0:T(8,128)(2,1)} async-done(((bf16[4,192,288]{2,1,0:T(8,128)(2,1)}), bf16[16,192,288]{2,1,0:T(8,128)(2,1)}) %all-gather.7.cloned.1.call-update) | async-done | bytes 1769488 | tf_op jit(solution)/shard_map/all_gather | solution.py:75
  150.2 1.2 slice_bitcast_fusion.39
  151.4 0.0 slice-start.4
  151.4 1.7 slice_bitcast_fusion.23
  153.1 0.0 slice-start.5
  153.1 3.1 %fusion.4 = f32[192,1792]{1,0:T(8,128)S(1)} fusion(bf16[4,1024,1792]{2,1,0:T(8,128)(2,1)} %param.19, bf16[192,256]{1,0:T(8,128)(2,1)S(1)} %get-tuple-element.34, bf16[192,256]{1,0:T(8,128)(2,1)S(1)} %get-tuple-element.35, bf16[192,256]{1,0:T(8,128)(2,1)S(1)} %get-tuple-element.36, bf16[192,256]{1,0:T(8,128)(2,1)S(1)} %get-tuple-element.25), kind=kOutput, calls=%fused_computation.5 | convolution fusion | flops 706215936 | bytes 5439488 | tf_op jit(solution)/shard_map/dot_general | solution.py:80
  156.2 0.4 fusion.39
  156.6 0.0 slice-start.6
  156.7 0.5 fusion.45
  157.1 3.1 %fusion = f32[192,1792]{1,0:T(8,128)S(1)} fusion(bf16[4,1024,1792]{2,1,0:T(8,128)(2,1)} %param.19, bf16[192,256]{1,0:T(8,128)(2,1)S(1)} %get-tuple-element.26, bf16[192,256]{1,0:T(8,128)(2,1)S(1)} %get-tuple-element.27, bf16[192,256]{1,0:T(8,128)(2,1)S(1)} %get-tuple-element.28, bf16[192,256]{1,0:T(8,128)(2,1)S(1)} %get-tuple-element.29), kind=kOutput, calls=%fused_computation.1 | convolution fusion | flops 706215936 | bytes 5439488 | tf_op jit(solution)/shard_map/dot_general | solution.py:80
  160.3 0.4 fusion.43
  160.7 0.5 fusion.47
  161.2 0.1 slice-done.7
  161.2 0.9 fusion.2
  162.1 0.4 fusion.41
  162.5 0.5 fusion.46
  163.0 0.9 fusion.6
  163.9 0.4 fusion.37
  164.3 0.5 fusion.44
  164.7 0.2 select_reduce_fusion.3
  165.0 31.3 %psum.7 = f32[256]{0:T(256)S(1)} all-reduce(f32[256]{0:T(256)S(1)} %add_multiply_fusion), channel_id=1, replica_groups=mesh['grp'=2,'exp'=4,'base'=4] {'exp','base'}, use_global_device_ids=true, to_apply=%region_11.12 | all-reduce | flops 256 | bytes 2048 | tf_op jit(solution)/shard_map/psum | solution.py:89
  196.3 0.6 dynamic_slice.3
  (35 shorter events, 0.1 us)
Async XLA Ops:
  7.4 54.8 %all-gather.5.cloned.1.call-start = ((), (), s32[]{:S(2)}) async-start(), calls=%async_computation.1 | async-start | bytes 4587520 | tf_op jit(solution)/shard_map/all_gather | solution.py:44
  30.8 3.2 %copy-start.1 = (bf16[64,7168]{1,0:T(8,128)(2,1)S(1)}, bf16[64,7168]{1,0:T(8,128)(2,1)}, u32[]{:S(2)}) copy-start(bf16[64,7168]{1,0:T(8,128)(2,1)} %all_gather.19) | copy-start | bytes 2752516
  30.8 69.4 %reduce-scatter.2.cloned.1.call-start = ((), (), s32[]{:S(2)}) async-start(), calls=%async_computation.2 | async-start | bytes 1146880 | tf_op jit(solution)/shard_map/reduce_scatter | solution.py:62
  34.0 6.9 %copy-start.6 = (s32[64,8]{0,1:T(8,128)S(1)}, s32[64,8]{0,1:T(8,128)}, u32[]{:S(2)}) copy-start(s32[64,8]{0,1:T(8,128)} %param.15) | copy-start | bytes 6148
  34.0 6.9 %copy-start.7 = (s32[64,8]{0,1:T(8,128)S(1)}, s32[64,8]{0,1:T(8,128)}, u32[]{:S(2)}) copy-start(s32[64,8]{0,1:T(8,128)} %param.14) | copy-start | bytes 6148
  34.0 28.2 %copy-start.2 = (bf16[4,7168,32]{1,2,0:T(8,128)(2,1)S(1)}, bf16[4,7168,32]{1,2,0:T(8,128)(2,1)}, u32[]{:S(2)}) copy-start(bf16[4,7168,32]{1,2,0:T(8,128)(2,1)} %param.20) | copy-start | bytes 5505028
  40.8 109.4 %all-gather.7.cloned.1.call-start = ((), (), s32[]{:S(2)}) async-start(), calls=%async_computation.3 | async-start | bytes 2949120 | tf_op jit(solution)/shard_map/all_gather | solution.py:75
  62.2 3.4 %copy-start = (bf16[256,7168]{1,0:T(8,128)(2,1)S(1)}, bf16[256,7168]{1,0:T(8,128)(2,1)}, u32[]{:S(2)}) copy-start(bf16[256,7168]{1,0:T(8,128)(2,1)} %all-gather.5.cloned.1.call-done) | copy-start | bytes 11010052
  65.6 3.8 %copy-start.3 = (bf16[4,7168,32]{1,2,0:T(8,128)(2,1)S(1)}, bf16[4,7168,32]{1,2,0:T(8,128)(2,1)}, u32[]{:S(2)}) copy-start(bf16[4,7168,32]{1,2,0:T(8,128)(2,1)} %param.21) | copy-start | bytes 5505028
  69.5 9.0 %slice-start = ((s8[14680064]{0:T(1024)(128)(4,1)}), s8[4194304]{0:T(1024)(128)(4,1)S(1)}, s32[]{:S(2)}) async-start(s8[14680064]{0:T(1024)(128)(4,1)} %bitcast.227), calls=%async_computation.4 | async-start | bytes 8388608
  70.7 7.8 %slice-start.1 = ((s8[14680064]{0:T(1024)(128)(4,1)}), s8[4194304]{0:T(1024)(128)(4,1)S(1)}, s32[]{:S(2)}) async-start(s8[14680064]{0:T(1024)(128)(4,1)} %bitcast.227), calls=%async_computation.5 | async-start | bytes 8388608
  70.7 7.8 %slice-start.2 = ((s8[14680064]{0:T(1024)(128)(4,1)}), s8[4194304]{0:T(1024)(128)(4,1)S(1)}, s32[]{:S(2)}) async-start(s8[14680064]{0:T(1024)(128)(4,1)} %bitcast.227), calls=%async_computation.6 | async-start | bytes 8388608
  76.0 2.5 %slice-start.3 = ((s8[14680064]{0:T(1024)(128)(4,1)}), s8[2097152]{0:T(1024)(128)(4,1)S(1)}, s32[]{:S(2)}) async-start(s8[14680064]{0:T(1024)(128)(4,1)} %bitcast.227), calls=%async_computation.7 | async-start | bytes 4194304
  151.4 9.8 %slice-start.4 = ((s8[14680064]{0:T(1024)(128)(4,1)}), s8[2097152]{0:T(1024)(128)(4,1)S(1)}, s32[]{:S(2)}) async-start(s8[14680064]{0:T(1024)(128)(4,1)} %bitcast.229), calls=%async_computation.8 | async-start | bytes 4194304
  153.1 3.1 %copy-start.4 = (bf16[4,128,1792]{2,1,0:T(8,128)(2,1)S(1)}, bf16[4,128,1792]{2,1,0:T(8,128)(2,1)}, u32[]{:S(2)}) copy-start(bf16[4,128,1792]{2,1,0:T(8,128)(2,1)} %param.22) | copy-start | bytes 5505028
  153.1 3.5 %copy-start.5 = (f32[1792]{0:T(1024)S(1)}, f32[1792]{0:T(1024)}, u32[]{:S(2)}) copy-start(f32[1792]{0:T(1024)} %param.16) | copy-start | bytes 21508
  153.1 8.0 %slice-start.5 = ((s8[14680064]{0:T(1024)(128)(4,1)}), s8[4194304]{0:T(1024)(128)(4,1)S(1)}, s32[]{:S(2)}) async-start(s8[14680064]{0:T(1024)(128)(4,1)} %bitcast.229), calls=%async_computation.9 | async-start | bytes 8388608
  156.6 4.5 %slice-start.6 = ((s8[14680064]{0:T(1024)(128)(4,1)}), s8[4194304]{0:T(1024)(128)(4,1)S(1)}, s32[]{:S(2)}) async-start(s8[14680064]{0:T(1024)(128)(4,1)} %bitcast.229), calls=%async_computation.10 | async-start | bytes 8388608
  157.1 4.1 %slice-start.7 = ((s8[14680064]{0:T(1024)(128)(4,1)}), s8[4194304]{0:T(1024)(128)(4,1)S(1)}, s32[]{:S(2)}) async-start(s8[14680064]{0:T(1024)(128)(4,1)} %bitcast.229), calls=%async_computation.11 | async-start | bytes 8388608
Sparse Core Ops, SparseCore 0:
  30.9 31.2 all-gather.4
Sparse Core Ops, SparseCore 1:
  40.9 24.4 reduce-scatter.1
  100.1 50.0 all-gather.6
where the time goes:
time: 205 us; the launch traced here: 204 us
  blocking collectives  70 us (34%)
  matrix products  58.1 us (28%)
  waiting for transfers between devices  55.4 us (27%)
  between operations  15.3 us (7%)
  local copies, waits for them, and re-layouts  3.8 us (2%)
    all_gather x1, waiting for transfers between devices, shards(): full = lax.all_gather(sent, 'base', axis=0, tiled=False)  40.2 us
    psum x1, blocking collectives, shards(): total = lax.psum(total / D, ('exp', 'base'))  31.3 us
    all_gather x1, blocking collectives, shards(): own_rows = lax.all_gather(tokens, 'base', axis=1, tiled=True)  23.4 us
    dot_general x8, matrix products, swiglu(): up_pre = jnp.dot(rows, up_w, preferred_element_type=jnp.float32)  20.1 us
    dot_general x9, matrix products, swiglu(): gate_pre = jnp.dot(rows, gate_w, preferred_element_type=jnp.float32)  18.7 us
    all_gather x1, waiting for transfers between devices, shards(): rows = lax.all_gather(own_rows, 'exp', axis=0, tiled=True)  15.2 us
    all_gather x1, blocking collectives, shards(): base_all = lax.all_gather(base_own, 'exp', axis=0, tiled=True)  9.8 us
    dot_general x4, matrix products, shards(): jnp.dot(hid, dense_down[j], preferred_element_type=jnp.float32)  7.97 us
  transfers between devices with their start and end apart: 3, of which 2 were waited for; matrix products, arithmetic and copies ran while one was open for 24% of the time, Pallas kernels for 0%

commit v1 on v0

--- a/solution.py
+++ b/solution.py
@@ -27,6 +27,13 @@
     base_up,
     base_down,
 ):
+
+    def _close_skins(target, frame_in):
+        left_arr = jnp.concatenate([target, frame_in], axis=1)
+        return jnp.split(
+            lax.all_gather(left_arr, "exp", axis=0, tiled=True), [target.shape[1]], axis=1
+        )
+
     groups = lax.axis_size("exp")
     splits = lax.axis_size("base")
     tok_rows, local_width = tokens.shape
@@ -41,7 +48,6 @@
         jnp.concatenate([expert_ids, gate_q], axis=1), "exp", axis=0, tiled=True
     )
     own_rows = lax.all_gather(tokens, "base", axis=1, tiled=True)
-    rows = lax.all_gather(own_rows, "exp", axis=0, tiled=True)
     ids, gates = (routing[:, :top_k], routing[:, top_k:])
     first = lax.axis_index("exp") * local_experts
     mine = first + jnp.arange(local_experts, dtype=jnp.int32)
@@ -62,7 +68,7 @@
     base_own = lax.psum_scatter(
         partial_value.astype(jnp.bfloat16), "base", scatter_dimension=1, tiled=True
     )
-    base_all = lax.all_gather(base_own, "exp", axis=0, tiled=True)
+    rows, base_all = _close_skins(own_rows, base_own)
     packed = []
     for j in range(local_experts):
         hidden = swiglu(rows, dense_gate[j], dense_up[j])

time: 205 us -> 271 us (1.32)
  waiting for transfers between devices: 55.4 us -> 105 us
  matrix products: 58.1 us -> 84.4 us
  blocking collectives: 70 us -> 59.7 us
    reduce_scatter x1, waiting for transfers between devices: 0.03 us -> 24.8 us  [shards(): lax.psum_scatter(partial_value.astype(jnp.bfloat16), 'base', scatter_dime...]
    all_gather x1, waiting for transfers between devices: 15.2 us -> 29.8 us  [_close_skins(): lax.all_gather(left_arr, 'exp', axis=0, tiled=True)]
    dot_general x9, matrix products: 18.7 us -> 32.5 us  [swiglu(): gate_pre = jnp.dot(rows, gate_w, preferred_element_type=jnp.float32)]
    all_gather x1, waiting for transfers between devices: 40.2 us -> 50.5 us  [shards(): full = lax.all_gather(sent, 'base', axis=0, tiled=False)]
    all_gather x1 -> x0, blocking collectives: 9.8 us -> none  [shards(): base_all = lax.all_gather(base_own, 'exp', axis=0, tiled=True)]
    dot_general x8, matrix products: 20.1 us -> 29 us  [swiglu(): up_pre = jnp.dot(rows, up_w, preferred_element_type=jnp.float32)]
    dot_general x4, matrix products: 7.97 us -> 11.9 us  [shards(): jnp.dot(hid, dense_down[j], preferred_element_type=jnp.float32)]
  transfers between devices with their start and end apart: 3 -> 3, of which waited for: 2 -> 3; matrix products, arithmetic and copies ran while one was open for 24% -> 0% of each run, Pallas kernels for 0% -> 0%
where the time goes in v1:
time: 271 us; the launch traced here: 270 us
  waiting for transfers between devices  105 us (39%)
  matrix products  84.4 us (31%)
  blocking collectives  59.7 us (22%)
  between operations  13.5 us (5%)
  local copies, waits for them, and re-layouts  4.05 us (1%)
  other arithmetic  3.55 us (1%)
    all_gather x1, waiting for transfers between devices, shards(): full = lax.all_gather(sent, 'base', axis=0, tiled=False)  50.5 us
    dot_general x9, matrix products, swiglu(): gate_pre = jnp.dot(rows, gate_w, preferred_element_type=jnp.float32)  32.5 us
    psum x1, blocking collectives, shards(): total = lax.psum(total / D, ('exp', 'base'))  31.3 us
    all_gather x1, waiting for transfers between devices, _close_skins(): lax.all_gather(left_arr, 'exp', axis=0, tiled=True)  29.8 us
    dot_general x8, matrix products, swiglu(): up_pre = jnp.dot(rows, up_w, preferred_element_type=jnp.float32)  29 us
    reduce_scatter x1, waiting for transfers between devices, shards(): lax.psum_scatter(partial_value.astype(jnp.bfloat16), 'base', scatter_dime...  24.8 us
    all_gather x1, blocking collectives, shards(): own_rows = lax.all_gather(tokens, 'base', axis=1, tiled=True)  23 us
    dot_general x4, matrix products, shards(): jnp.dot(hid, dense_down[j], preferred_element_type=jnp.float32)  11.9 us
  transfers between devices with their start and end apart: 3, of which 3 were waited for; matrix products, arithmetic and copies ran while one was open for 0% of the time, Pallas kernels for 0%

profile of v1, /device:TPU:0, one launch (start us, length us, event | category | flops | bytes accessed | tf_op | source)
XLA Modules:
  0.0 270.4 jit_solution(386038696704940868)
XLA Ops:
  6.5 23.0 %all_gather.16 = bf16[64,7168]{1,0:T(8,128)(2,1)S(1)} all-gather(bf16[64,1792]{1,0:T(8,128)(2,1)} %param.13), channel_id=1, replica_groups=mesh['grp'=2,'exp'=4,'base'=4] {'base'}, dimensions={1}, use_global_device_ids=true | all-gather | bytes 1146880 | tf_op jit(solution)/shard_map/all_gather | solution.py:50
  29.5 2.7 %fusion.226 = f32[64,256]{1,0:T(8,128)S(1)} fusion(bf16[64,7168]{1,0:T(8,128)(2,1)S(1)} %all_gather.16, bf16[7168,256]{1,0:T(8,128)(2,1)} %param.23), kind=kOutput, calls=%fused_computation.288 | convolution fusion | flops 234881024 | bytes 4653056 | tf_op jit(solution)/shard_map/dot_general | solution.py:10
  32.2 6.4 %convolution_convert_fusion = bf16[64,7168]{1,0:T(8,128)(2,1)} fusion(bf16[256,7168]{1,0:T(8,128)(2,1)} %param.25, bf16[64,7168]{1,0:T(8,128)(2,1)S(1)} %all_gather.16, bf16[7168,256]{1,0:T(8,128)(2,1)} %param.24, f32[64,256]{1,0:T(8,128)S(1)} %fusion.226), kind=kOutput, calls=%fused_computation | convolution fusion | flops 470319104 | bytes 9240576 | tf_op jit(solution)/shard_map/dot_general | solution.py:67
  38.6 0.0 reduce-scatter.2.cloned.1.call-update
  38.7 0.0 all-gather.5.cloned.1.call-start
  38.7 24.8 %reduce-scatter.2.cloned.1.call-done = bf16[64,1792]{1,0:T(8,128)(2,1)} async-done(((bf16[64,7168]{1,0:T(8,128)(2,1)}), bf16[64,1792]{1,0:T(8,128)(2,1)}) %reduce-scatter.2.cloned.1.call-update) | async-done | bytes 229392 | tf_op jit(solution)/shard_map/reduce_scatter | solution.py:68
  63.5 2.1 pad_maximum_fusion
  65.5 0.0 all-gather.5.cloned.1.call-update
  65.6 0.0 all-gather.7.cloned.1.call-start
  65.6 5.4 %all-gather.1 = s32[4,64,16]{1,2,0:T(8,128)S(1)} all-gather(s32[1,64,16]{1,2,0:T(8,128)S(1)} %add_bitcast_fusion), channel_id=1, replica_groups=mesh['grp'=2,'exp'=4,'base'=4] {'exp'}, dimensions={0}, use_global_device_ids=true | all-gather | bytes 20480 | tf_op jit(solution)/shard_map/all_gather | solution.py:47
  71.0 0.1 reshape.45
  71.1 0.1 compare_reduce_fusion
  71.2 0.2 fusion.82
  71.5 0.1 iota_compare_fusion
  71.6 29.8 %all-gather.5.cloned.1.call-done = bf16[256,8960]{1,0:T(8,128)(2,1)} async-done(((bf16[64,8960]{1,0:T(8,128)(2,1)}), bf16[256,8960]{1,0:T(8,128)(2,1)}) %all-gather.5.cloned.1.call-update) | async-done | bytes 4587536 | tf_op jit(solution)/shard_map/all_gather | solution.py:34
  101.4 3.4 %fusion.98 = f32[256,32]{0,1:T(8,128)S(1)} fusion(bf16[4,7168,32]{1,2,0:T(8,128)(2,1)S(1)} %copy-done.4, bf16[256,8960]{1,0:T(8,128)(2,1)} %all-gather.5.cloned.1.call-done), kind=kOutput, calls=%fused_computation.108 | convolution fusion | flops 117440512 | bytes 4161536 | tf_op jit(solution)/shard_map/dot_general | solution.py:10
  104.7 0.0 slice-start
  104.8 0.0 slice-start.1
  104.8 5.5 %fusion.18 = f32[256,256]{0,1:T(8,128)S(1)} fusion(bf16[4,7168,256]{2,1,0:T(8,128)(2,1)} %param.17, bf16[256,8960]{1,0:T(8,128)(2,1)} %all-gather.5.cloned.1.call-done), kind=kOutput, calls=%fused_computation.19 | convolution fusion | flops 939524096 | bytes 7602176 | tf_op jit(solution)/shard_map/dot_general | solution.py:10
  110.3 4.1 %fusion.78 = bf16[256,32]{0,1:T(8,128)(2,1)S(1)} fusion(bf16[4,7168,32]{1,2,0:T(8,128)(2,1)} %param.21, f32[256,32]{0,1:T(8,128)S(1)} %fusion.98, bf16[256,8960]{1,0:T(8,128)(2,1)} %all-gather.5.cloned.1.call-done), kind=kOutput, calls=%fused_computation.85 | convolution fusion | flops 117489664 | bytes 4177920 | tf_op jit(solution)/shard_map/dot_general | solution.py:11
  114.3 0.0 slice-start.2
  114.4 0.0 slice-start.3
  114.4 3.9 %fusion.66 = bf16[256,256]{0,1:T(8,128)(2,1)S(1)} fusion(bf16[4,7168,256]{2,1,0:T(8,128)(2,1)S(1)} %copy-done.3, f32[256,256]{0,1:T(8,128)S(1)} %fusion.18, bf16[256,8960]{1,0:T(8,128)(2,1)} %all-gather.5.cloned.1.call-done), kind=kOutput, calls=%fused_computation.71 | convolution fusion | flops 939917312 | bytes 7733248 | tf_op jit(solution)/shard_map/dot_general | solution.py:11
  118.2 0.2 fusion.73
  118.5 3.2 %fusion.95 = f32[256,32]{0,1:T(8,128)S(1)} fusion(bf16[4,7168,32]{1,2,0:T(8,128)(2,1)S(1)} %copy-done.4, bf16[256,8960]{1,0:T(8,128)(2,1)} %all-gather.5.cloned.1.call-done), kind=kOutput, calls=%fused_computation.105 | convolution fusion | flops 117440512 | bytes 4161536 | tf_op jit(solution)/shard_map/dot_general | solution.py:10
  121.7 0.0 slice-done
  121.8 3.7 %fusion.14 = f32[256,256]{0,1:T(8,128)S(1)} fusion(bf16[4,7168,256]{2,1,0:T(8,128)(2,1)S(1)} %bitcast.208, bf16[256,8960]{1,0:T(8,128)(2,1)} %all-gather.5.cloned.1.call-done), kind=kOutput, calls=%fused_computation.15 | convolution fusion | flops 939524096 | bytes 7602176 | tf_op jit(solution)/shard_map/dot_general | solution.py:10
  125.4 3.3 %fusion.79 = bf16[256,32]{0,1:T(8,128)(2,1)S(1)} fusion(bf16[4,7168,32]{1,2,0:T(8,128)(2,1)} %param.21, f32[256,32]{0,1:T(8,128)S(1)} %fusion.95, bf16[256,8960]{1,0:T(8,128)(2,1)} %all-gather.5.cloned.1.call-done), kind=kOutput, calls=%fused_computation.86 | convolution fusion | flops 117489664 | bytes 4177920 | tf_op jit(solution)/shard_map/dot_general | solution.py:11
  128.8 3.7 %fusion.63 = bf16[256,256]{0,1:T(8,128)(2,1)S(1)} fusion(bf16[4,7168,256]{2,1,0:T(8,128)(2,1)S(1)} %copy-done.3, f32[256,256]{0,1:T(8,128)S(1)} %fusion.14, bf16[256,8960]{1,0:T(8,128)(2,1)} %all-gather.5.cloned.1.call-done), kind=kOutput, calls=%fused_computation.70 | convolution fusion | flops 939917312 | bytes 7733248 | tf_op jit(solution)/shard_map/dot_general | solution.py:11
  132.5 0.2 fusion.74
  132.7 3.2 %fusion.92 = f32[256,32]{0,1:T(8,128)S(1)} fusion(bf16[4,7168,32]{1,2,0:T(8,128)(2,1)S(1)} %copy-done.4, bf16[256,8960]{1,0:T(8,128)(2,1)} %all-gather.5.cloned.1.call-done), kind=kOutput, calls=%fused_computation.102 | convolution fusion | flops 117440512 | bytes 4161536 | tf_op jit(solution)/shard_map/dot_general | solution.py:10
  135.9 3.9 %fusion.10 = f32[256,256]{0,1:T(8,128)S(1)} fusion(bf16[4,7168,256]{2,1,0:T(8,128)(2,1)S(1)} %bitcast.208, bf16[256,8960]{1,0:T(8,128)(2,1)} %all-gather.5.cloned.1.call-done), kind=kOutput, calls=%fused_computation.11 | convolution fusion | flops 939524096 | bytes 7602176 | tf_op jit(solution)/shard_map/dot_general | solution.py:10
  139.8 3.3 %fusion.80 = bf16[256,32]{0,1:T(8,128)(2,1)S(1)} fusion(bf16[4,7168,32]{1,2,0:T(8,128)(2,1)} %param.21, f32[256,32]{0,1:T(8,128)S(1)} %fusion.92, bf16[256,8960]{1,0:T(8,128)(2,1)} %all-gather.5.cloned.1.call-done), kind=kOutput, calls=%fused_computation.87 | convolution fusion | flops 117489664 | bytes 4177920 | tf_op jit(solution)/shard_map/dot_general | solution.py:11
  143.2 3.7 %fusion.60 = bf16[256,256]{0,1:T(8,128)(2,1)S(1)} fusion(bf16[4,7168,256]{2,1,0:T(8,128)(2,1)S(1)} %copy-done.3, f32[256,256]{0,1:T(8,128)S(1)} %fusion.10, bf16[256,8960]{1,0:T(8,128)(2,1)} %all-gather.5.cloned.1.call-done), kind=kOutput, calls=%fused_computation.69 | convolution fusion | flops 939917312 | bytes 7733248 | tf_op jit(solution)/shard_map/dot_general | solution.py:11
  146.9 0.2 fusion.75
  147.1 3.2 %fusion.101 = f32[256,32]{0,1:T(8,128)S(1)} fusion(bf16[4,7168,32]{1,2,0:T(8,128)(2,1)S(1)} %copy-done.4, bf16[256,8960]{1,0:T(8,128)(2,1)} %all-gather.5.cloned.1.call-done), kind=kOutput, calls=%fused_computation.111 | convolution fusion | flops 117440512 | bytes 4161536 | tf_op jit(solution)/shard_map/dot_general | solution.py:10
  150.4 3.7 %fusion.22 = f32[256,256]{0,1:T(8,128)S(1)} fusion(bf16[4,7168,256]{2,1,0:T(8,128)(2,1)S(1)} %bitcast.208, bf16[256,8960]{1,0:T(8,128)(2,1)} %all-gather.5.cloned.1.call-done), kind=kOutput, calls=%fused_computation.23 | convolution fusion | flops 939524096 | bytes 7602176 | tf_op jit(solution)/shard_map/dot_general | solution.py:10
  154.0 3.3 %fusion.77 = bf16[256,32]{0,1:T(8,128)(2,1)S(1)} fusion(bf16[4,7168,32]{1,2,0:T(8,128)(2,1)} %param.21, f32[256,32]{0,1:T(8,128)S(1)} %fusion.101, bf16[256,8960]{1,0:T(8,128)(2,1)} %all-gather.5.cloned.1.call-done), kind=kOutput, calls=%fused_computation.84 | convolution fusion | flops 117489664 | bytes 4177920 | tf_op jit(solution)/shard_map/dot_general | solution.py:11
  157.4 3.7 %fusion.69 = bf16[256,256]{0,1:T(8,128)(2,1)S(1)} fusion(bf16[4,7168,256]{2,1,0:T(8,128)(2,1)S(1)} %copy-done.3, f32[256,256]{0,1:T(8,128)S(1)} %fusion.22, bf16[256,8960]{1,0:T(8,128)(2,1)} %all-gather.5.cloned.1.call-done), kind=kOutput, calls=%fused_computation.72 | convolution fusion | flops 939917312 | bytes 7733248 | tf_op jit(solution)/shard_map/dot_general | solution.py:11
  161.1 0.2 fusion.72
  161.3 1.0 pad_maximum_fusion.1
  162.3 0.0 all-gather.7.cloned.1.call-update
  162.3 0.1 fusion.193
  162.4 50.5 %all-gather.7.cloned.1.call-done = bf16[16,192,288]{2,1,0:T(8,128)(2,1)} async-done(((bf16[4,192,288]{2,1,0:T(8,128)(2,1)}), bf16[16,192,288]{2,1,0:T(8,128)(2,1)}) %all-gather.7.cloned.1.call-update) | async-done | bytes 1769488 | tf_op jit(solution)/shard_map/all_gather | solution.py:81
  213.0 1.2 slice_bitcast_fusion.39
  214.1 1.6 slice_bitcast_fusion.23
  215.7 2.9 %fusion.4 = f32[192,1792]{1,0:T(8,128)S(1)} fusion(bf16[4,1024,1792]{2,1,0:T(8,128)(2,1)} %param.19, bf16[192,256]{1,0:T(8,128)(2,1)S(1)} %get-tuple-element.34, bf16[192,256]{1,0:T(8,128)(2,1)S(1)} %get-tuple-element.35, bf16[192,256]{1,0:T(8,128)(2,1)S(1)} %get-tuple-element.36, bf16[192,256]{1,0:T(8,128)(2,1)S(1)} %get-tuple-element.25), kind=kOutput, calls=%fused_computation.5 | convolution fusion | flops 706215936 | bytes 5439488 | tf_op jit(solution)/shard_map/dot_general | solution.py:86
  218.6 2.9 %fusion = f32[192,1792]{1,0:T(8,128)S(1)} fusion(bf16[4,1024,1792]{2,1,0:T(8,128)(2,1)} %param.19, bf16[192,256]{1,0:T(8,128)(2,1)S(1)} %get-tuple-element.26, bf16[192,256]{1,0:T(8,128)(2,1)S(1)} %get-tuple-element.27, bf16[192,256]{1,0:T(8,128)(2,1)S(1)} %get-tuple-element.28, bf16[192,256]{1,0:T(8,128)(2,1)S(1)} %get-tuple-element.29), kind=kOutput, calls=%fused_computation.1 | convolution fusion | flops 706215936 | bytes 5439488 | tf_op jit(solution)/shard_map/dot_general | solution.py:86
  221.6 2.9 %fusion.2 = f32[192,1792]{1,0:T(8,128)S(1)} fusion(bf16[4,1024,1792]{2,1,0:T(8,128)(2,1)} %param.19, bf16[192,256]{1,0:T(8,128)(2,1)S(1)} %get-tuple-element.30, bf16[192,256]{1,0:T(8,128)(2,1)S(1)} %get-tuple-element.31, bf16[192,256]{1,0:T(8,128)(2,1)S(1)} %get-tuple-element.32, bf16[192,256]{1,0:T(8,128)(2,1)S(1)} %get-tuple-element.33), kind=kOutput, calls=%fused_computation.3 | convolution fusion | flops 706215936 | bytes 5439488 | tf_op jit(solution)/shard_map/dot_general | solution.py:86
  224.5 0.0 copy-start
  224.6 3.1 %fusion.6 = f32[192,1792]{1,0:T(8,128)S(1)} fusion(bf16[4,1024,1792]{2,1,0:T(8,128)(2,1)} %param.19, bf16[192,256]{1,0:T(8,128)(2,1)S(1)} %get-tuple-element.37, bf16[192,256]{1,0:T(8,128)(2,1)S(1)} %get-tuple-element.38, bf16[192,256]{1,0:T(8,128)(2,1)S(1)} %get-tuple-element.39, bf16[192,256]{1,0:T(8,128)(2,1)S(1)} %get-tuple-element.40), kind=kOutput, calls=%fused_computation.7 | convolution fusion | flops 706215936 | bytes 5439488 | tf_op jit(solution)/shard_map/dot_general | solution.py:86
  227.7 0.4 fusion.39
  228.1 0.4 fusion.43
  228.5 0.0 copy-start.5
  228.5 0.4 fusion.41
  228.9 0.4 fusion.37
  229.3 0.5 slice-done.5
  229.9 0.5 fusion.45
  230.3 0.5 fusion.47
  230.8 0.5 fusion.46
  231.3 0.5 fusion.44
  231.7 0.2 select_reduce_fusion.3
  231.9 31.3 %psum.7 = f32[256]{0:T(256)S(1)} all-reduce(f32[256]{0:T(256)S(1)} %add_multiply_fusion), channel_id=1, replica_groups=mesh['grp'=2,'exp'=4,'base'=4] {'exp','base'}, use_global_device_ids=true, to_apply=%region_11.12 | all-reduce | flops 256 | bytes 2048 | tf_op jit(solution)/shard_map/psum | solution.py:95
  263.3 0.6 dynamic_slice.3
  (27 shorter events, 0.1 us)
Async XLA Ops:
  6.5 56.9 %reduce-scatter.2.cloned.1.call-start = ((), (), s32[]{:S(2)}) async-start(), calls=%async_computation.1 | async-start | bytes 1146880 | tf_op jit(solution)/shard_map/reduce_scatter | solution.py:68
  38.6 27.0 %copy-start.1 = (s32[64,8]{0,1:T(8,128)S(1)}, s32[64,8]{0,1:T(8,128)}, u32[]{:S(2)}) copy-start(s32[64,8]{0,1:T(8,128)} %param.15) | copy-start | bytes 6148
  38.6 27.0 %copy-start.2 = (s32[64,8]{0,1:T(8,128)S(1)}, s32[64,8]{0,1:T(8,128)}, u32[]{:S(2)}) copy-start(s32[64,8]{0,1:T(8,128)} %param.14) | copy-start | bytes 6148
  38.6 62.7 %copy-start.4 = (bf16[4,7168,32]{1,2,0:T(8,128)(2,1)S(1)}, bf16[4,7168,32]{1,2,0:T(8,128)(2,1)}, u32[]{:S(2)}) copy-start(bf16[4,7168,32]{1,2,0:T(8,128)(2,1)} %param.20) | copy-start | bytes 5505028
  38.7 62.7 %all-gather.5.cloned.1.call-start = ((), (), s32[]{:S(2)}) async-start(), calls=%async_computation.2 | async-start | bytes 5734400 | tf_op jit(solution)/shard_map/all_gather | solution.py:34
  65.6 147.4 %all-gather.7.cloned.1.call-start = ((), (), s32[]{:S(2)}) async-start(), calls=%async_computation.3 | async-start | bytes 2949120 | tf_op jit(solution)/shard_map/all_gather | solution.py:81
  101.4 13.0 %copy-start.3 = (bf16[4,7168,256]{2,1,0:T(8,128)(2,1)S(1)}, bf16[4,7168,256]{2,1,0:T(8,128)(2,1)}, u32[]{:S(2)}) copy-start(bf16[4,7168,256]{2,1,0:T(8,128)(2,1)} %param.18) | copy-start | bytes 44040196
  104.7 17.0 %slice-start = ((s8[14680064]{0:T(1024)(128)(4,1)}), s8[4194304]{0:T(1024)(128)(4,1)S(1)}, s32[]{:S(2)}) async-start(s8[14680064]{0:T(1024)(128)(4,1)} %bitcast.207), calls=%async_computation.4 | async-start | bytes 8388608
  104.8 16.9 %slice-start.1 = ((s8[14680064]{0:T(1024)(128)(4,1)}), s8[4194304]{0:T(1024)(128)(4,1)S(1)}, s32[]{:S(2)}) async-start(s8[14680064]{0:T(1024)(128)(4,1)} %bitcast.207), calls=%async_computation.5 | async-start | bytes 8388608
  114.3 7.4 %slice-start.2 = ((s8[14680064]{0:T(1024)(128)(4,1)}), s8[4194304]{0:T(1024)(128)(4,1)S(1)}, s32[]{:S(2)}) async-start(s8[14680064]{0:T(1024)(128)(4,1)} %bitcast.207), calls=%async_computation.6 | async-start | bytes 8388608
  114.4 7.4 %slice-start.3 = ((s8[14680064]{0:T(1024)(128)(4,1)}), s8[2097152]{0:T(1024)(128)(4,1)S(1)}, s32[]{:S(2)}) async-start(s8[14680064]{0:T(1024)(128)(4,1)} %bitcast.207), calls=%async_computation.7 | async-start | bytes 4194304
  224.5 3.1 %copy-start = (bf16[4,128,1792]{2,1,0:T(8,128)(2,1)S(1)}, bf16[4,128,1792]{2,1,0:T(8,128)(2,1)}, u32[]{:S(2)}) copy-start(bf16[4,128,1792]{2,1,0:T(8,128)(2,1)} %param.22) | copy-start | bytes 5505028
  224.6 4.8 %slice-start.4 = ((s8[4587520]{0:T(1024)(128)(4,1)}), s8[393216]{0:T(1024)(128)(4,1)S(1)}, s32[]{:S(2)}) async-start(s8[4587520]{0:T(1024)(128)(4,1)} %bitcast.209), calls=%async_computation.8 | async-start | bytes 786432
  227.7 2.2 slice-start.5
  228.5 1.4 copy-start.5
Sparse Core Ops, SparseCore 0:
  38.8 24.6 reduce-scatter.1
  65.7 35.6 all-gather.4
  162.4 50.4 all-gather.6
